TPU v7x, 256 devices: a whole 4x4x8 slice. The times are simulated.
256 devices in a mesh: row: 8 (over y, core), leaf: 32 (over x, z).
Axes of the slice: x: 4, y: 4, z: 8, core: 2. Of those that a mesh axis runs over, the one named last changes fastest.
Arguments:
- diag_blocks: float32 [32, 24, 256, 256], P('leaf', 'row'), as said below
- panel: float32 [32, 24, 768, 256], P('leaf', None, 'row'), may hold values from -1.5 to 1.5
- parent: int32 [32, 24, 1], replicated, may hold values from 0 to 31; in each aligned block of 24 rows (0 to 23, 24 to 47, ..., all dimensions but the last counted through in order) at most 2 rows name the same one
- rel: int32 [32, 24, 6], replicated, may hold values from 0 to 7, as said below
- front: float32 [32, 1024, 1024], P('leaf', None, 'row'), may hold values from -6 to 6
Outputs:
- factor_diag: float32 [32, 24, 256, 256], P('leaf', 'row')
- factor_panel: bfloat16 [32, 24, 768, 256], P('leaf', None, 'row')
- new_front: float32 [32, 1024, 1024], P('leaf', None, 'row')
Inputs may be any that keep to these rules, and one draw needn't show every extreme that they name: Among the 24 supernodes of one leaf index at most 2 have the same parent owner, and some leaf index reaches 2. `rel`: the 6 entries of each supernode name different blocks of the parent's front, in rising order. `diag_blocks`: every block is symmetric positive definite.
All inputs are finite; a program needn't handle non-finite values.
Results may differ from a plain program's by a relative error of at most 0.0011.
Values may be sent and summed in bfloat16 or wider, within the bound.
No kernel may reach another device: no remote copies, remote signals or barrier semaphores. Data moves between devices by JAX's collectives and lax.ppermute only.
A program may use at most 128 MiB of HBM per device.

v0:
```python
import jax
import jax.numpy as jnp
from jax import lax
from jax.sharding import PartitionSpec as P

W = 256
BS = 128
FB = 8
P_SIZE = 6


def on_device(diag_blocks, panel, parent, rel, front):
    row_count = lax.axis_size("row")
    leaf_count = lax.axis_size("leaf")
    row_index = lax.axis_index("row")
    leaf_index = lax.axis_index("leaf")
    own_factor = jnp.linalg.cholesky(diag_blocks[0])
    factors_all = lax.all_gather(own_factor, "row", axis=0, tiled=True)
    solved = jax.scipy.linalg.solve_triangular(
        factors_all, jnp.swapaxes(panel[0], 1, 2), lower=True
    )
    panel_rows = jnp.swapaxes(solved, 1, 2).astype(jnp.bfloat16)
    owners = parent[:, :, 0]
    supernodes = owners.shape[1]
    most_slots = max(2, 3 * supernodes // (2 * leaf_count))
    node_ids = jnp.arange(supernodes, dtype=jnp.int32)
    before = node_ids[None, :] < node_ids[:, None]
    same_owner = owners[:, :, None] == owners[:, None, :]
    position = jnp.sum(jnp.logical_and(same_owner, before[None]), axis=2)
    slot_ids = jnp.arange(most_slots, dtype=jnp.int32)
    targets = jnp.arange(leaf_count, dtype=jnp.int32)
    my_owner = lax.dynamic_index_in_dim(owners, leaf_index, 0, keepdims=False)
    my_position = lax.dynamic_index_in_dim(position, leaf_index, 0, keepdims=False)
    send_match = jnp.logical_and(
        my_owner[None, None, :] == targets[:, None, None],
        my_position[None, None, :] == slot_ids[None, :, None],
    )
    send_child = jnp.sum(jnp.where(send_match, node_ids, 0), axis=2)
    send_valid = jnp.any(send_match, axis=2)
    recv_match = jnp.logical_and(
        owners[:, None, :] == leaf_index, position[:, None, :] == slot_ids[None, :, None]
    )
    recv_valid = jnp.any(recv_match, axis=2)
    recv_blocks = jnp.sum(jnp.where(recv_match[..., None], rel[:, None, :, :], 0), axis=2)
    blocks_per_row = FB // row_count
    owned_blocks = row_index * blocks_per_row + jnp.arange(blocks_per_row, dtype=jnp.int32)
    columns = blocks_per_row * BS
    full_panel = lax.all_gather(panel_rows, "row", axis=1, tiled=True)
    my_blocks = lax.dynamic_index_in_dim(rel, leaf_index, 0, keepdims=False)
    leading = full_panel.shape[:-2]
    selector = (my_blocks[..., None, :] == owned_blocks[:, None]).astype(jnp.bfloat16)
    parted = full_panel.reshape(leading + (P_SIZE, BS, W))
    picked = jnp.einsum(
        "...tp,...pbw->...tbw", selector, parted, preferred_element_type=jnp.float32
    ).astype(jnp.bfloat16)
    picked = picked.reshape(leading + (columns, W))
    child_updates = jnp.einsum(
        "...iw,...cw->...ic", full_panel, picked, preferred_element_type=jnp.float32
    ).astype(jnp.bfloat16)
    outgoing = jnp.where(
        send_valid[..., None, None],
        jnp.take(child_updates, send_child, axis=0),
        jnp.zeros((), jnp.bfloat16),
    )
    incoming = lax.all_to_all(outgoing, "leaf", split_axis=0, concat_axis=0, tiled=True)
    front_ids = jnp.arange(FB, dtype=jnp.int32)
    placing = jnp.logical_and(
        recv_blocks[..., None, :] == front_ids[:, None], recv_valid[..., None, None]
    ).astype(jnp.bfloat16)
    parted_updates = incoming.reshape(incoming.shape[0], incoming.shape[1], P_SIZE, BS, columns)
    assembled = jnp.einsum(
        "smfp,smpic->fic", placing, parted_updates, preferred_element_type=jnp.float32
    )
    new_front = front[0] - assembled.reshape(FB * BS, columns)
    return (own_factor[None], panel_rows[None], new_front[None])


def solution(mesh):
    in_specs = (
        P("leaf", "row", None, None),
        P("leaf", None, "row", None),
        P(),
        P(),
        P("leaf", None, "row"),
    )
    out_specs = (P("leaf", "row", None, None), P("leaf", None, "row", None), P("leaf", None, "row"))
    return jax.shard_map(
        on_device, mesh=mesh, in_specs=in_specs, out_specs=out_specs, check_vma=False
    )
```

profile of v0, /device:TPU:163, one launch (start us, length us, event | category | flops | bytes accessed | tf_op | source)
XLA Modules:
  0.0 1087.2 jit_solution(9359395064277232795)
XLA Ops:
  7.3 1.4 copy.66
  8.7 1.2 fusion.16
  10.0 35.2 %custom-call.17 = f32[3,128,128]{2,1,0:T(8,128)S(1)} custom-call(f32[3,128,128]{2,1,0:T(8,128)S(1)} %cholesky.122), custom_call_target="Cholesky" | custom-call | tf_op jit(solution)/shard_map/jit(cholesky)/cholesky | solution.py:17
  45.2 29.5 %custom-call.18 = f32[3,1,128,128]{2,3,1,0:T(8,128)S(1)} custom-call(f32[3,1,128,128]{3,2,1,0:T(8,128)S(1)} %select_bitcast_fusion), custom_call_target="InvertDiagBlocksLowerTriangular" | custom-call | tf_op jit(solution)/shard_map/jit(cholesky)/cholesky | solution.py:17
  74.7 0.1 cholesky.117
  74.7 0.3 constant_dynamic-update-slice_fusion.1
  75.1 0.5 convolution_subtract_fusion
  75.6 35.2 %custom-call.19 = f32[3,128,128]{2,1,0:T(8,128)S(1)} custom-call(f32[3,128,128]{2,1,0:T(8,128)S(1)} %convolution_subtract_fusion), custom_call_target="Cholesky" | custom-call | tf_op jit(solution)/shard_map/jit(cholesky)/cholesky | solution.py:17
  110.8 0.1 compare_reduce_fusion
  111.0 1.0 select_select_fusion.1
  112.1 0.0 all-gather.5.cloned.1.call-start
  112.1 45.1 %all-gather.3.cloned.1.call-done = f32[24,256,256]{2,1,0:T(8,128)} async-done(((f32[3,256,256]{2,1,0:T(8,128)}), f32[24,256,256]{2,1,0:T(8,128)}) %all-gather.3.cloned.1.call-update) | async-done | bytes 6291472 | tf_op jit(solution)/shard_map/all_gather | solution.py:18
  157.3 6.3 broadcast_select_fusion
  163.6 0.1 triangular_solve.48
  163.7 10.5 while.1
  163.7 0.6 fusion.41
  164.3 5.0 bitcast_dynamic-update-slice_fusion.2
  169.3 0.6 fusion.41
  169.8 4.4 bitcast_dynamic-update-slice_fusion.2
  174.2 473.0 %custom-call.20 = f32[24,2,128,128]{2,3,1,0:T(8,128)} custom-call(f32[24,2,128,128]{3,2,1,0:T(8,128)} %bitcast.90), custom_call_target="InvertDiagBlocksLowerTriangular" | custom-call | tf_op jit(solution)/shard_map/jit(_solve_triangular)/vmap()/triangular_solve | solution.py:19
  647.2 2.9 fusion.32
  650.1 4.9 fusion.8
  655.1 1.5 fusion.11
  656.7 1.7 fusion.18
  658.4 0.2 convert_reduce_fusion
  658.6 0.2 dynamic-slice_reduce_fusion
  658.8 0.6 dynamic-slice_reduce_fusion.1
  659.4 0.1 iota_compare_fusion.5
  659.5 0.1 fusion.25
  659.6 0.1 copy.74
  659.7 0.1 and_reduce_fusion
  659.8 0.1 copy.73
  659.9 0.1 copy.76
  660.0 0.1 reshape.180
  660.1 0.1 constant_dynamic-slice_fusion.1
  660.2 0.1 copy.90
  660.3 0.1 copy.82
  660.5 54.8 %all-gather.5.cloned.1.call-done = bf16[24,768,256]{2,1,0:T(8,128)(2,1)} async-done(((bf16[24,96,256]{2,1,0:T(8,128)(2,1)}), bf16[24,768,256]{2,1,0:T(8,128)(2,1)}) %all-gather.5.cloned.1.call-update) | async-done | bytes 9437200 | tf_op jit(solution)/shard_map/all_gather | solution.py:48
  715.3 11.9 %fusion = bf16[24,1,128,256]{3,1,2,0:T(2,128)(2,1)} fusion(pred[24,6,1,1]{1,2,3,0:T(4,128)(4,1)S(1)} %copy.82, bf16[24,6,128,256]{3,2,1,0:T(8,128)(2,1)} %bitcast.84), kind=kOutput, calls=%fused_computation.3 | convolution fusion | flops 9437184 | bytes 11010192 | tf_op jit(solution)/shard_map/...tp,...pbw->...tbw/dot_general | solution.py:53
  727.2 6.1 convolution_convert_fusion
  733.3 9.5 gather_fusion
  742.8 11.0 %select_select_fusion = bf16[32,2,768,128]{3,2,1,0:T(8,128)(2,1)} fusion(bf16[32,2,768,128]{3,2,1,0:T(8,128)(2,1)} %bitcast.83, pred[32,2]{1,0:T(8,128)(4,1)S(1)} %copy.74, pred[32,2]{1,0:T(8,128)(4,1)S(1)} %copy.73), kind=kLoop, calls=%fused_computation.7 | loop fusion | flops 12582912 | bytes 25165952 | tf_op jit(solution)/shard_map/jit(_where)/select_n | solution.py:60
  753.9 9.2 all-to-all-start
  763.1 1.0 fusion.39
  764.2 302.4 %all-to-all-done = bf16[32,2,768,128]{3,2,1,0:T(8,128)(2,1)} async-done(((bf16[32,2,768,128]{3,2,1,0:T(8,128)(2,1)}), bf16[32,2,768,128]{3,2,1,0:T(8,128)(2,1)}, u32[]{:S(2)}, u32[]{:S(2)}) %all-to-all-start) | async-done | bytes 12582944 | tf_op jit(solution)/shard_map/all_to_all | solution.py:65
  1066.6 12.8 %fusion.12 = f32[8,128,128]{2,0,1:T(8,128)S(1)} fusion(bf16[32,2,6,128,128]{4,3,2,1,0:T(8,128)(2,1)} %bitcast.24, s32[32,2,6]{0,2,1:T(8,128)S(1)} %select_reduce_fusion.2, pred[32,2]{0,1:T(4,128)(4,1)S(1)} %get-tuple-element.21), kind=kOutput, calls=%fused_computation.19 | convolution fusion | flops 100669440 | bytes 13108800 | tf_op jit(solution)/shard_map/smfp,smpic->fic/dot_general | solution.py:71
  1079.4 0.1 copy.78
  1079.5 0.9 bitcast_subtract_fusion
  (35 shorter events, 0.4 us)
Async XLA Ops:
  7.2 150.1 %all-gather.3.cloned.1.call-start = ((), (), s32[]{:S(2)}) async-start(), calls=%async_computation.1 | async-start | bytes 7077888 | tf_op jit(solution)/shard_map/all_gather | solution.py:18
  112.1 603.2 %all-gather.5.cloned.1.call-start = ((), (), s32[]{:S(2)}) async-start(), calls=%async_computation.2 | async-start | bytes 10616832 | tf_op jit(solution)/shard_map/all_gather | solution.py:48
  163.7 483.5 %copy-start.2 = (f32[1,24,96,256]{3,2,1,0:T(8,128)S(1)}, f32[1,24,96,256]{3,2,1,0:T(8,128)}, u32[]{:S(2)}) copy-start(f32[1,24,96,256]{3,2,1,0:T(8,128)} %param.6) | copy-start | bytes 7077892
  650.1 5.0 copy-start.1
  656.6 1.8 copy-start.5
  656.7 3.4 copy-start.4
  715.3 11.9 %copy-start = (bf16[24,768,256]{2,1,0:T(8,128)(2,1)S(1)}, bf16[24,768,256]{2,1,0:T(8,128)(2,1)}, u32[]{:S(2)}) copy-start(bf16[24,768,256]{2,1,0:T(8,128)(2,1)} %all-gather.5.cloned.1.call-done) | copy-start | bytes 28311556
  753.9 312.7 %all-to-all-start = ((bf16[32,2,768,128]{3,2,1,0:T(8,128)(2,1)}), bf16[32,2,768,128]{3,2,1,0:T(8,128)(2,1)}, u32[]{:S(2)}, u32[]{:S(2)}) async-start(bf16[32,2,768,128]{3,2,1,0:T(8,128)(2,1)} %select_select_fusion), calls=%async_computation | async-start | bytes 25165824 | tf_op jit(solution)/shard_map/all_to_all | solution.py:65
  1066.6 12.9 %copy-start.3 = (f32[1,1024,128]{2,1,0:T(8,128)S(1)}, f32[1,1024,128]{2,1,0:T(8,128)}, u32[]{:S(2)}) copy-start(f32[1,1024,128]{2,1,0:T(8,128)} %param.9) | copy-start | bytes 1572868
Sparse Core Ops, SparseCore 0:
  112.2 45.0 all-gather.2
  658.5 56.7 all-gather.4
where the time goes:
time: 1090 us
  other arithmetic  597 us (55%)
  waiting for transfers between devices  402 us (37%)
  matrix products  41.1 us (4%)
  local copies, waits for them, and re-layouts  23.2 us (2%)
  between operations  14.3 us (1%)
    another operation x3, other arithmetic, on_device(): jax.scipy.linalg.solve_triangular(factors_all, jnp.swapaxes(panel[0], 1,...  479 us
    all_to_all x1, waiting for transfers between devices, on_device(): lax.all_to_all(outgoing, 'leaf', split_axis=0, concat_axis=0, tiled=True)  302 us
    another operation x9, other arithmetic, on_device(): own_factor = jnp.linalg.cholesky(diag_blocks[0])  100 us
    all_gather x1, waiting for transfers between devices, on_device(): full_panel = lax.all_gather(panel_rows, 'row', axis=1, tiled=True)  54.8 us
    all_gather x1, waiting for transfers between devices, on_device(): factors_all = lax.all_gather(own_factor, 'row', axis=0, tiled=True)  45.1 us
  transfers between devices with their start and end apart: 3, of which 3 were waited for; matrix products, arithmetic and copies ran while one was open for 0% of the time, Pallas kernels for 0%

commit v1 on v0

--- a/solution.py
+++ b/solution.py
@@ -45,7 +45,8 @@
     blocks_per_row = FB // row_count
     owned_blocks = row_index * blocks_per_row + jnp.arange(blocks_per_row, dtype=jnp.int32)
     columns = blocks_per_row * BS
-    full_panel = lax.all_gather(panel_rows, "row", axis=1, tiled=True)
+    copies = jnp.concatenate([panel_rows] * lax.axis_size("row"), axis=1)
+    full_panel = lax.all_to_all(copies, "row", 1, 1, tiled=True)
     my_blocks = lax.dynamic_index_in_dim(rel, leaf_index, 0, keepdims=False)
     leading = full_panel.shape[:-2]
     selector = (my_blocks[..., None, :] == owned_blocks[:, None]).astype(jnp.bfloat16)

time: 1090 us -> 1180 us (1.083)
  the two profiles are of different devices: /device:TPU:163 before, /device:TPU:179 now
where the time goes in v1:
time: 1180 us; the launch traced here: 1170 us
  other arithmetic  606 us (51%)
  waiting for transfers between devices  449 us (38%)
  matrix products  50.1 us (4%)
  local copies, waits for them, and re-layouts  36.2 us (3%)
  starting transfers between devices  15.9 us (1%)
  between operations  14.7 us (1%)
    another operation x3, other arithmetic, on_device(): jax.scipy.linalg.solve_triangular(factors_all, jnp.swapaxes(panel[0], 1,...  479 us
    all_to_all x1, waiting for transfers between devices, on_device(): lax.all_to_all(outgoing, 'leaf', split_axis=0, concat_axis=0, tiled=True)  305 us
    all_to_all x1, waiting for transfers between devices, on_device(): full_panel = lax.all_to_all(copies, 'row', 1, 1, tiled=True)  100 us
    another operation x9, other arithmetic, on_device(): own_factor = jnp.linalg.cholesky(diag_blocks[0])  100 us
    all_gather x1, waiting for transfers between devices, on_device(): factors_all = lax.all_gather(own_factor, 'row', axis=0, tiled=True)  43.8 us
  transfers between devices with their start and end apart: 3, of which 3 were waited for; matrix products, arithmetic and copies ran while one was open for 0% of the time, Pallas kernels for 0%

profile of v1, /device:TPU:179, one launch (start us, length us, event | category | flops | bytes accessed | tf_op | source)
XLA Modules:
  0.0 1172.2 jit_solution(12195322814132007092)
XLA Ops:
  7.3 1.4 copy.70
  8.7 1.2 fusion.21
  10.0 35.2 %custom-call.17 = f32[3,128,128]{2,1,0:T(8,128)S(1)} custom-call(f32[3,128,128]{2,1,0:T(8,128)S(1)} %cholesky.122), custom_call_target="Cholesky" | custom-call | tf_op jit(solution)/shard_map/jit(cholesky)/cholesky | solution.py:17
  45.2 29.5 %custom-call.18 = f32[3,1,128,128]{2,3,1,0:T(8,128)S(1)} custom-call(f32[3,1,128,128]{3,2,1,0:T(8,128)S(1)} %select_bitcast_fusion), custom_call_target="InvertDiagBlocksLowerTriangular" | custom-call | tf_op jit(solution)/shard_map/jit(cholesky)/cholesky | solution.py:17
  74.7 0.3 constant_dynamic-update-slice_fusion.1
  75.1 0.5 convolution_subtract_fusion
  75.6 35.2 %custom-call.19 = f32[3,128,128]{2,1,0:T(8,128)S(1)} custom-call(f32[3,128,128]{2,1,0:T(8,128)S(1)} %convolution_subtract_fusion), custom_call_target="Cholesky" | custom-call | tf_op jit(solution)/shard_map/jit(cholesky)/cholesky | solution.py:17
  110.8 0.1 compare_reduce_fusion
  111.0 1.0 select_select_fusion.1
  112.1 43.8 %all-gather.2.cloned.1.call-done = f32[24,256,256]{2,1,0:T(8,128)} async-done(((f32[3,256,256]{2,1,0:T(8,128)}), f32[24,256,256]{2,1,0:T(8,128)}) %all-gather.2.cloned.1.call-update) | async-done | bytes 6291472 | tf_op jit(solution)/shard_map/all_gather | solution.py:18
  155.9 6.3 broadcast_select_fusion
  162.3 10.4 while.1
  162.3 0.6 fusion.44
  162.9 4.9 bitcast_dynamic-update-slice_fusion.10
  167.7 0.6 fusion.44
  168.3 4.4 bitcast_dynamic-update-slice_fusion.10
  172.7 473.2 %custom-call.20 = f32[24,2,128,128]{2,3,1,0:T(8,128)} custom-call(f32[24,2,128,128]{3,2,1,0:T(8,128)} %bitcast.95), custom_call_target="InvertDiagBlocksLowerTriangular" | custom-call | tf_op jit(solution)/shard_map/jit(_solve_triangular)/vmap()/triangular_solve | solution.py:19
  645.8 3.2 fusion.36
  649.1 5.3 fusion.13
  654.4 1.5 fusion.16
  655.9 1.2 bitcast_dynamic-update-slice_fusion.7
  657.1 1.2 bitcast_dynamic-update-slice_fusion.6
  658.3 1.3 bitcast_dynamic-update-slice_fusion.5
  659.6 1.2 bitcast_dynamic-update-slice_fusion.4
  660.8 1.2 bitcast_dynamic-update-slice_fusion.3
  662.0 1.2 bitcast_dynamic-update-slice_fusion.2
  663.2 1.2 bitcast_dynamic-update-slice_fusion.1
  664.4 1.2 bitcast_dynamic-update-slice_fusion.8
  665.6 12.9 %copy.79 = bf16[24,768,256]{2,0,1:T(8,128)(2,1)} copy(bf16[24,768,256]{2,1,0:T(8,128)(2,1)} %bitcast_dynamic-update-slice_fusion.8) | data formatting | bytes 18874368 | tf_op jit(solution)/shard_map/concatenate | solution.py:48
  678.5 6.7 all-to-all-start
  685.2 0.2 convert_reduce_fusion
  685.4 0.2 dynamic-slice_reduce_fusion
  685.6 0.6 dynamic-slice_reduce_fusion.1
  686.6 0.1 copy.77
  686.8 0.1 reshape.180
  687.0 0.1 copy.96
  687.1 0.1 copy.88
  687.2 100.4 %all-to-all-done = bf16[24,768,256]{2,0,1:T(8,128)(2,1)} async-done(((bf16[24,768,256]{2,0,1:T(8,128)(2,1)}), bf16[24,768,256]{2,0,1:T(8,128)(2,1)}, u32[]{:S(2)}, u32[]{:S(2)}) %all-to-all-start) | async-done | bytes 9437216 | tf_op jit(solution)/shard_map/all_to_all | solution.py:49
  787.7 17.9 %fusion = bf16[24,1,128,256]{3,1,2,0:T(2,128)(2,1)S(1)} fusion(pred[24,6,1,1]{1,2,3,0:T(4,128)(4,1)S(1)} %copy.88, bf16[24,6,128,256]{3,0,2,1:T(8,128)(2,1)} %bitcast.20), kind=kOutput, calls=%fused_computation.3 | convolution fusion | flops 9437184 | bytes 11010192 | tf_op jit(solution)/shard_map/...tp,...pbw->...tbw/dot_general | solution.py:54
  805.6 8.4 fusion.6
  814.0 9.7 gather_fusion
  823.7 11.0 select_select_fusion
  834.8 9.2 all-to-all-start.1
  844.0 1.0 fusion.42
  845.1 1.2 fusion.32
  846.3 304.8 %all-to-all-done.1 = bf16[32,2,768,128]{3,2,1,0:T(8,128)(2,1)} async-done(((bf16[32,2,768,128]{3,2,1,0:T(8,128)(2,1)}), bf16[32,2,768,128]{3,2,1,0:T(8,128)(2,1)}, u32[]{:S(2)}, u32[]{:S(2)}) %all-to-all-start.1) | async-done | bytes 12582944 | tf_op jit(solution)/shard_map/all_to_all | solution.py:66
  1151.1 12.8 %fusion.17 = f32[8,128,128]{2,0,1:T(8,128)S(1)} fusion(bf16[32,2,6,128,128]{4,3,2,1,0:T(8,128)(2,1)} %bitcast.24, s32[32,2,6]{0,2,1:T(8,128)S(1)} %select_reduce_fusion.2, pred[32,2]{0,1:T(4,128)(4,1)S(1)} %get-tuple-element.21), kind=kOutput, calls=%fused_computation.21 | convolution fusion | flops 100669440 | bytes 13108800 | tf_op jit(solution)/shard_map/smfp,smpic->fic/dot_general | solution.py:72
  1164.1 0.9 bitcast_subtract_fusion
  (39 shorter events, 1.1 us)
Async XLA Ops:
  7.2 148.7 %all-gather.2.cloned.1.call-start = ((), (), s32[]{:S(2)}) async-start(), calls=%async_computation.2 | async-start | bytes 7077888 | tf_op jit(solution)/shard_map/all_gather | solution.py:18
  649.1 5.3 copy-start
  678.5 6.7 copy-start.3
  678.5 8.4 copy-start.2
  678.5 109.2 %all-to-all-start = ((bf16[24,768,256]{2,0,1:T(8,128)(2,1)}), bf16[24,768,256]{2,0,1:T(8,128)(2,1)}, u32[]{:S(2)}, u32[]{:S(2)}) async-start(bf16[24,768,256]{2,0,1:T(8,128)(2,1)} %copy.79), calls=%async_computation | async-start | bytes 18874368 | tf_op jit(solution)/shard_map/all_to_all | solution.py:49
  834.8 316.3 %all-to-all-start.1 = ((bf16[32,2,768,128]{3,2,1,0:T(8,128)(2,1)}), bf16[32,2,768,128]{3,2,1,0:T(8,128)(2,1)}, u32[]{:S(2)}, u32[]{:S(2)}) async-start(bf16[32,2,768,128]{3,2,1,0:T(8,128)(2,1)} %select_select_fusion), calls=%async_computation.1 | async-start | bytes 25165824 | tf_op jit(solution)/shard_map/all_to_all | solution.py:66
  1151.1 12.9 %copy-start.1 = (f32[1,1024,128]{2,1,0:T(8,128)S(1)}, f32[1,1024,128]{2,1,0:T(8,128)}, u32[]{:S(2)}) copy-start(f32[1,1024,128]{2,1,0:T(8,128)} %param.9) | copy-start | bytes 1572868
Sparse Core Ops, SparseCore 0:
  112.2 43.6 all-gather.1
